TPU v7x, 512 devices: a whole 4x8x8 slice. The times are simulated.
512 devices in a mesh: dom: 64 (over y, x, core), feat: 8 (over z).
Axes of the slice: x: 4, y: 8, z: 8, core: 2. Of those that a mesh axis runs over, the one named last changes fastest.
Arguments:
- features: bfloat16 [512, 196608], P('feat', 'dom'), may hold values from -16 to 16
- weights: bfloat16 [2, 512, 512], replicated, may hold values from -0.1875 to 0.1875
- tile_values: bfloat16 [4608, 128, 128], P('dom'), may hold values from 0 to 0.099609375
- tile_blocks: int32 [4608, 2], P('dom'), may hold values from 0 to 31
- tile_counts: int32 [64], P('dom'), may hold values from 36 to 72
- replica: int32 [64, 64, 16], P('dom'), may hold values from -1 to 3071, as said below
- cotangent: bfloat16 [512, 196608], P(None, ('dom', 'feat')), may hold values from -6 to 6
Outputs:
- output: bfloat16 [512, 196608], P(None, ('dom', 'feat'))
- feature_grad: bfloat16 [512, 196608], P('feat', 'dom')
- weight_grad: float32 [2, 512, 512], P(None, 'feat')
Inputs may be any that keep to these rules, and one draw needn't show every extreme that they name: `tile_blocks`: column 0 names a tile's source block and column 1 its destination block. replica[q, p, k] is the master slot on partition q of the vertex in mirror slot q * 16 + k of partition p, or -1 for an unused slot; the used slots of a pair (q, p) come first; no partition mirrors its own masters; each master partition fills all 16 slots toward at least one partition.
All inputs are finite; a program needn't handle non-finite values.
Results may differ from a plain program's by a relative error of at most 0.0058.
Values may be sent and summed in bfloat16 or wider, within the bound.
A program may use at most 64 MiB of HBM per device.

v0:
```python
import jax
import jax.numpy as jnp
from jax import lax
from jax.sharding import PartitionSpec as P


def gathered_total(x, axis):
    pieces = lax.all_gather(x, axis).astype(jnp.float32)
    return pieces.sum(axis=0)


def local(features, weights, tile_values, tile_blocks, tile_counts, replica, cotangent):
    feat_width, masters = features.shape
    tile_size = tile_values.shape[1]
    replica_rows = replica[0]
    slot_used = (replica_rows >= 0).reshape(-1)
    slot_index = jnp.where(replica_rows >= 0, replica_rows, 0).reshape(-1)
    tile_live = (jnp.arange(tile_values.shape[0]) < tile_counts[0]).astype(jnp.float32)
    source_blocks = tile_blocks[:, 0]
    target_blocks = tile_blocks[:, 1]

    def pull_mirrors(values_in):
        outgoing = jnp.where(
            slot_used[None, :],
            jnp.take(values_in, slot_index, axis=1),
            jnp.zeros((), values_in.dtype),
        )
        return lax.all_to_all(outgoing, "dom", split_axis=1, concat_axis=1, tiled=True)

    def push_mirrors(partial_value):
        incoming = lax.all_to_all(
            partial_value[:, masters:].astype(jnp.bfloat16),
            "dom",
            split_axis=1,
            concat_axis=1,
            tiled=True,
        ).astype(jnp.float32)
        targets = jnp.where(slot_used, slot_index, masters)
        return partial_value[:, :masters].at[:, targets].add(incoming, mode="drop")

    def spread(own_cols, forward):
        local_cols = jnp.concatenate([own_cols, pull_mirrors(own_cols)], 1)
        nblocks = local_cols.shape[1] // tile_size
        blocks = local_cols.reshape(feat_width, nblocks, tile_size)
        if forward:
            picked = jnp.take(blocks, source_blocks, axis=1)
            contrib = jnp.einsum(
                "fts,tsd->ftd", picked, tile_values, preferred_element_type=jnp.float32
            )
            segment = target_blocks
        else:
            picked = jnp.take(blocks, target_blocks, axis=1)
            contrib = jnp.einsum(
                "ftd,tsd->fts", picked, tile_values, preferred_element_type=jnp.float32
            )
            segment = source_blocks
        onehot = (segment[:, None] == jnp.arange(nblocks)[None, :]).astype(jnp.float32) * tile_live[
            :, None
        ]
        partial_value = jnp.einsum("ftd,tb->fbd", contrib, onehot, precision=lax.Precision.HIGHEST)
        return push_mirrors(partial_value.reshape(feat_width, nblocks * tile_size))

    aggregate = spread(features, True).astype(jnp.bfloat16)
    feat_rows, agg_rows = (
        lax.all_to_all(features, "feat", split_axis=1, concat_axis=0, tiled=True),
        lax.all_to_all(aggregate, "feat", split_axis=1, concat_axis=0, tiled=True),
    )
    preact = jnp.einsum("io,iv->ov", weights[0], feat_rows, preferred_element_type=jnp.float32)
    preact = preact + jnp.einsum(
        "io,iv->ov", weights[1], agg_rows, preferred_element_type=jnp.float32
    )
    sigmoid_z = jax.nn.sigmoid(preact)
    output = (preact * sigmoid_z).astype(jnp.bfloat16)
    slope = sigmoid_z * (1.0 + preact * (1.0 - sigmoid_z))
    pre_grad = (cotangent.astype(jnp.float32) * slope).astype(jnp.bfloat16)
    slice_start = lax.axis_index("feat") * feat_width
    grad_cols = lax.all_gather(pre_grad, "feat", axis=1, tiled=True)
    weight_slice = lax.dynamic_slice_in_dim(weights, slice_start, feat_width, 1)
    terms = jnp.stack(
        [
            jnp.einsum("iv,ov->io", features, grad_cols, preferred_element_type=jnp.float32),
            jnp.einsum("iv,ov->io", aggregate, grad_cols, preferred_element_type=jnp.float32),
        ]
    )
    weight_grad = gathered_total(terms.astype(jnp.bfloat16), "dom").astype(jnp.float32)
    back_slices = jnp.einsum(
        "kio,ov->kiv", weight_slice, grad_cols, preferred_element_type=jnp.float32
    ).astype(jnp.bfloat16)
    self_grad = back_slices[0]
    agg_grad = back_slices[1]
    back_terms = spread(agg_grad, False)
    feature_grad = (self_grad.astype(jnp.float32) + back_terms).astype(jnp.bfloat16)
    return (output, feature_grad, weight_grad)


def solution(mesh):
    return jax.shard_map(
        local,
        mesh=mesh,
        in_specs=(
            P("feat", "dom"),
            P(),
            P("dom", None, None),
            P("dom", None),
            P("dom"),
            P("dom", None, None),
            P(None, ("dom", "feat")),
        ),
        out_specs=(P(None, ("dom", "feat")), P("feat", "dom"), P(None, "feat", None)),
        check_vma=False,
    )
```

profile of v0, /device:TPU:1, one launch (start us, length us, event | category | flops | bytes accessed | tf_op | source)
XLA Modules:
  0.0 258.0 jit_solution(7112404868492813658)
XLA Ops:
  7.2 0.9 copy.71
  8.2 0.5 copy-done.6
  8.8 1.4 copy.72
  10.1 4.3 %gather_fusion = bf16[1024,64]{1,0:T(8,128)(2,1)} fusion(bf16[64,3072]{0,1:T(8,128)(2,1)S(1)} %copy.72, s32[1024]{0:T(1024)S(1)} %fusion.34), kind=kCustom, calls=%fused_computation.clone | custom fusion | bytes 266240 | tf_op jit(solution)/shard_map/jit(_take)/gather | solution.py:25
  14.5 1.3 bitcast_select_fusion.1
  15.8 0.8 reshape.201
  16.6 11.6 %all-to-all-start.1 = ((bf16[64,2,512]{2,1,0:T(2,128)(2,1)}), bf16[64,2,512]{2,1,0:T(2,128)(2,1)S(1)}, u32[]{:S(2)}, u32[]{:S(2)}) async-start(bf16[64,2,512]{2,1,0:T(2,128)(2,1)} %reshape.201), calls=%async_computation.1 | async-start | bytes 262144 | tf_op jit(solution)/shard_map/all_to_all | solution.py:28
  28.2 0.5 compare_and_fusion.1
  29.5 1.3 slice_bitcast_fusion.2
  30.8 8.6 %all-to-all-done.1 = bf16[64,2,512]{2,1,0:T(2,128)(2,1)S(1)} async-done(((bf16[64,2,512]{2,1,0:T(2,128)(2,1)}), bf16[64,2,512]{2,1,0:T(2,128)(2,1)S(1)}, u32[]{:S(2)}, u32[]{:S(2)}) %all-to-all-start.1) | async-done | bytes 131104 | tf_op jit(solution)/shard_map/all_to_all | solution.py:28
  39.3 0.2 reshape.202
  39.7 0.1 copy_bitcast_fusion.3
  39.9 1.8 gather_fusion.1
  41.7 2.1 convolution_bitcast_fusion.1
  43.8 2.7 %fusion.3 = f32[32,64,128]{2,0,1:T(8,128)S(1)} fusion(f32[64,72,128]{2,0,1:T(8,128)S(1)} %convolution_bitcast_fusion.1, f32[72]{0:T(128)S(1)} %compare_convert_fusion, s32[72]{0:T(128)S(1)} %get-tuple-element.29), kind=kOutput, calls=%fused_computation.11 | convolution fusion | flops 226497024 | bytes 3408448 | tf_op jit(solution)/shard_map/ftd,tb->fbd/dot_general | solution.py:60
  46.4 0.6 copy.104
  47.1 1.0 copy-done.3
  48.1 0.2 copy.77
  48.2 0.8 reshape.203
  49.1 4.4 %all-to-all-start.2 = ((bf16[64,2,512]{2,1,0:T(2,128)(2,1)}), bf16[64,2,512]{2,1,0:T(2,128)(2,1)S(1)}, u32[]{:S(2)}, u32[]{:S(2)}) async-start(bf16[64,2,512]{2,1,0:T(2,128)(2,1)} %reshape.203), calls=%async_computation.2 | async-start | bytes 262144 | tf_op jit(solution)/shard_map/all_to_all | solution.py:31
  53.6 0.8 copy.105
  54.3 10.6 %all-to-all-done.2 = bf16[64,2,512]{2,1,0:T(2,128)(2,1)S(1)} async-done(((bf16[64,2,512]{2,1,0:T(2,128)(2,1)}), bf16[64,2,512]{2,1,0:T(2,128)(2,1)S(1)}, u32[]{:S(2)}, u32[]{:S(2)}) %all-to-all-start.2) | async-done | bytes 131104 | tf_op jit(solution)/shard_map/all_to_all | solution.py:31
  64.9 10.0 %all-to-all-start = ((bf16[64,8,384]{2,0,1:T(8,128)(2,1)}), bf16[64,8,384]{2,0,1:T(8,128)(2,1)}, u32[]{:S(2)}, u32[]{:S(2)}) async-start(bf16[64,8,384]{2,0,1:T(8,128)(2,1)} %bitcast.122), calls=%async_computation | async-start | bytes 786432 | tf_op jit(solution)/shard_map/all_to_all | solution.py:65
  75.0 0.6 compare_select_fusion
  75.6 1.2 slice.50
  76.8 1.6 copy.78
  78.5 1.1 reshape.204
  79.6 8.2 %scatter_custom_fusion = f32[64,3072]{0,1:T(8,128)} fusion(f32[64,3072]{0,1:T(8,128)} %copy.78, s32[1024]{0:T(1024)} %bitcast.140, bf16[64,1024]{0,1:T(8,128)(2,1)S(1)} %bitcast.133), kind=kCustom, calls=%fused_computation.42 | custom fusion | flops 131072 | bytes 917504 | tf_op jit(solution)/shard_map/scatter-add | solution.py:39
  87.8 1.5 convert_element_type.61
  89.3 1.0 copy.79
  90.3 6.6 %all-to-all-start.3 = ((bf16[64,8,384]{2,0,1:T(8,128)(2,1)}), bf16[64,8,384]{2,0,1:T(8,128)(2,1)}, u32[]{:S(2)}, u32[]{:S(2)}) async-start(bf16[64,8,384]{2,0,1:T(8,128)(2,1)} %copy.79), calls=%async_computation.3 | async-start | bytes 786432 | tf_op jit(solution)/shard_map/all_to_all | solution.py:66
  96.9 0.2 all-gather.3.cloned.1.call-start
  97.1 2.5 fusion.19
  99.7 10.7 %all-to-all-done.3 = bf16[64,8,384]{2,0,1:T(8,128)(2,1)} async-done(((bf16[64,8,384]{2,0,1:T(8,128)(2,1)}), bf16[64,8,384]{2,0,1:T(8,128)(2,1)}, u32[]{:S(2)}, u32[]{:S(2)}) %all-to-all-start.3) | async-done | bytes 393248 | tf_op jit(solution)/shard_map/all_to_all | solution.py:66
  110.4 3.1 %multiply_convert_fusion = (bf16[512,384]{1,0:T(8,128)(2,1)}, bf16[512,384]{1,0:T(8,128)(2,1)}) fusion(bf16[512,384]{1,0:T(8,128)(2,1)} %param.17, f32[512,384]{1,0:T(8,128)} %fusion.19, bf16[512,384]{1,0:T(8,128)(2,1)} %bitcast.19, bf16[2,512,512]{2,1,0:T(8,128)(2,1)} %param.12), kind=kOutput, calls=%fused_computation.30 | convolution fusion | flops 203882496 | bytes 2883584 | tf_op jit(solution)/shard_map/io,iv->ov/dot_general | solution.py:69
  113.6 38.6 %all-gather.3.cloned.1.call-done = bf16[512,3072]{1,0:T(8,128)(2,1)} async-done(((bf16[512,384]{1,0:T(8,128)(2,1)}), bf16[512,3072]{1,0:T(8,128)(2,1)}) %all-gather.3.cloned.1.call-update) | async-done | bytes 3145744 | tf_op jit(solution)/shard_map/all_gather | solution.py:77
  152.2 3.1 %fusion.13 = bf16[1,1,64,512]{3,2,1,0:T(8,128)(2,1)S(1)} fusion(bf16[64,3072]{0,1:T(8,128)(2,1)S(1)} %convert_element_type.61, bf16[512,3072]{1,0:T(8,128)(2,1)} %all-gather.3.cloned.1.call-done), kind=kOutput, calls=%fused_computation.26 | convolution fusion | flops 201359360 | bytes 3604480 | tf_op jit(solution)/shard_map/iv,ov->io/dot_general | solution.py:82
  155.3 1.1 fusion.12
  156.4 0.7 pad_maximum_fusion
  157.1 2.6 convolution_convert_fusion
  159.7 0.9 copy-done.4
  160.6 0.4 copy.81
  161.0 4.3 %gather_fusion.2 = bf16[1024,64]{1,0:T(8,128)(2,1)} fusion(bf16[64,3072]{0,1:T(8,128)(2,1)S(1)} %copy.81, s32[1024]{0:T(1024)S(1)} %fusion.34), kind=kCustom, calls=%fused_computation.2.clone | custom fusion | bytes 266240 | tf_op jit(solution)/shard_map/jit(_take)/gather | solution.py:25
  165.3 1.3 bitcast_select_fusion
  166.6 0.2 reshape.205
  166.8 23.0 %all_to_all.80 = bf16[64,2,512]{2,1,0:T(2,128)(2,1)S(1)} all-to-all(bf16[64,2,512]{2,1,0:T(2,128)(2,1)S(1)} %reshape.205), channel_id=1, replica_groups=mesh['dom'=64,'feat'=8] {'dom'}, dimensions={0} | all-to-all | bytes 262144 | tf_op jit(solution)/shard_map/all_to_all | solution.py:28
  189.7 0.2 reshape.206
  190.1 0.1 copy_bitcast_fusion.2
  190.2 1.9 gather_fusion.3
  192.1 3.0 %convolution_bitcast_fusion = f32[64,72,128]{2,0,1:T(8,128)S(1)} fusion(bf16[72,128,128]{2,1,0:T(8,128)(2,1)S(1)} %copy-done, bf16[72,64,128]{2,1,0:T(8,128)(2,1)} %gather_fusion.3, pred[72]{0:T(512)(128)(4,1)S(1)} %copy-done.11), kind=kOutput, calls=%fused_computation.13 | convolution fusion | flops 151584768 | bytes 5898312 | tf_op jit(solution)/shard_map/ftd,tsd->fts/dot_general | solution.py:53
  195.1 2.7 %fusion.1 = f32[32,64,128]{2,0,1:T(8,128)S(1)} fusion(f32[64,72,128]{2,0,1:T(8,128)S(1)} %convolution_bitcast_fusion, s32[72]{0:T(128)S(1)} %copy-done.12, f32[72]{0:T(128)S(1)} %copy-done.10), kind=kOutput, calls=%fused_computation.9 | convolution fusion | flops 226497024 | bytes 3408448 | tf_op jit(solution)/shard_map/ftd,tb->fbd/dot_general | solution.py:60
  197.8 0.6 copy.103
  198.4 0.8 copy.85
  199.3 1.8 reshape.207
  201.0 4.5 %all-to-all-start.5 = ((bf16[64,2,512]{2,1,0:T(2,128)(2,1)}), bf16[64,2,512]{2,1,0:T(2,128)(2,1)S(1)}, u32[]{:S(2)}, u32[]{:S(2)}) async-start(bf16[64,2,512]{2,1,0:T(2,128)(2,1)} %reshape.207), calls=%async_computation.5 | async-start | bytes 262144 | tf_op jit(solution)/shard_map/all_to_all | solution.py:31
  205.5 1.9 slice_add_fusion
  207.5 2.8 %copy.86 = f32[64,3072]{0,1:T(8,128)} copy(f32[64,3072]{1,0:T(8,128)} %slice_add_fusion) | data formatting | bytes 1572864 | tf_op jit(solution)/shard_map/add
  210.3 6.6 %all-to-all-done.5 = bf16[64,2,512]{2,1,0:T(2,128)(2,1)S(1)} async-done(((bf16[64,2,512]{2,1,0:T(2,128)(2,1)}), bf16[64,2,512]{2,1,0:T(2,128)(2,1)S(1)}, u32[]{:S(2)}, u32[]{:S(2)}) %all-to-all-start.5) | async-done | bytes 131104 | tf_op jit(solution)/shard_map/all_to_all | solution.py:31
  216.9 0.2 reshape.208
  217.1 8.2 %scatter_custom_fusion.1 = f32[64,3072]{0,1:T(8,128)} fusion(f32[64,3072]{0,1:T(8,128)} %copy.86, s32[1024]{0:T(1024)} %bitcast.141, bf16[64,1024]{0,1:T(8,128)(2,1)S(1)} %bitcast.132), kind=kCustom, calls=%fused_computation.40 | custom fusion | flops 131072 | bytes 917504 | tf_op jit(solution)/shard_map/scatter-add | solution.py:39
  225.3 1.5 convert_element_type.70
  226.8 1.0 copy.87
  227.8 17.9 %all-gather.5.cloned.1.call-done = bf16[64,2,64,512]{3,2,1,0:T(8,128)(2,1)} async-done(((bf16[1,2,64,512]{3,2,1,0:T(8,128)(2,1)}), bf16[64,2,64,512]{3,2,1,0:T(8,128)(2,1)}) %all-gather.5.cloned.1.call-update) | async-done | bytes 8388624 | tf_op jit(solution)/shard_map/all_gather | solution.py:8
  245.7 5.5 %convert_reduce_fusion = f32[2,64,512]{2,1,0:T(8,128)} fusion(bf16[64,2,64,512]{3,2,1,0:T(8,128)(2,1)} %all-gather.5.cloned.1.call-done), kind=kLoop, calls=%fused_computation.6 | loop fusion | flops 8323072 | bytes 8650752 | tf_op jit(solution)/shard_map/reduce_sum | solution.py:9
  (38 shorter events, 0.6 us)
Async XLA Ops:
  7.2 34.5 %copy-start = (bf16[72,128,128]{2,1,0:T(8,128)(2,1)S(1)}, bf16[72,128,128]{2,1,0:T(8,128)(2,1)}, u32[]{:S(2)}) copy-start(bf16[72,128,128]{2,1,0:T(8,128)(2,1)} %param.13) | copy-start | bytes 7077892
  7.2 32.5 %copy-start.2 = (bf16[64,3072]{1,0:T(8,128)(2,1)S(1)}, bf16[64,3072]{1,0:T(8,128)(2,1)}, u32[]{:S(2)}) copy-start(bf16[64,3072]{1,0:T(8,128)(2,1)} %param.11) | copy-start | bytes 1179652
  7.2 21.0 %copy-start.8 = (s32[72,2]{0,1:T(2,128)S(1)}, s32[72,2]{0,1:T(2,128)}, u32[]{:S(2)}) copy-start(s32[72,2]{0,1:T(2,128)} %param.14) | copy-start | bytes 1732
  8.1 0.6 copy-start.6
  16.6 22.7 %all-to-all-start.1 = ((bf16[64,2,512]{2,1,0:T(2,128)(2,1)}), bf16[64,2,512]{2,1,0:T(2,128)(2,1)S(1)}, u32[]{:S(2)}, u32[]{:S(2)}) async-start(bf16[64,2,512]{2,1,0:T(2,128)(2,1)} %reshape.201), calls=%async_computation.1 | async-start | bytes 262144 | tf_op jit(solution)/shard_map/all_to_all | solution.py:28
  29.5 14.3 %copy-start.9 = (f32[72]{0:T(128)}, f32[72]{0:T(128)S(1)}, u32[]{:S(2)}) copy-start(f32[72]{0:T(128)S(1)} %compare_convert_fusion) | copy-start | bytes 868
  46.4 28.5 %copy-start.7 = (s32[1,64,16]{2,1,0:T(8,128)S(1)}, s32[1,64,16]{2,1,0:T(8,128)}, u32[]{:S(2)}) copy-start(s32[1,64,16]{2,1,0:T(8,128)} %copy-done.6) | copy-start | bytes 12292
  47.1 1.0 copy-start.3
  49.1 15.8 %all-to-all-start.2 = ((bf16[64,2,512]{2,1,0:T(2,128)(2,1)}), bf16[64,2,512]{2,1,0:T(2,128)(2,1)S(1)}, u32[]{:S(2)}, u32[]{:S(2)}) async-start(bf16[64,2,512]{2,1,0:T(2,128)(2,1)} %reshape.203), calls=%async_computation.2 | async-start | bytes 262144 | tf_op jit(solution)/shard_map/all_to_all | solution.py:31
  64.9 10.1 %copy-start.5 = (bf16[64,2,512]{2,1,0:T(2,128)(2,1)}, bf16[64,2,512]{2,1,0:T(2,128)(2,1)S(1)}, u32[]{:S(2)}) copy-start(bf16[64,2,512]{2,1,0:T(2,128)(2,1)S(1)} %all-to-all-done.2) | copy-start | bytes 393220
  64.9 25.4 %all-to-all-start = ((bf16[64,8,384]{2,0,1:T(8,128)(2,1)}), bf16[64,8,384]{2,0,1:T(8,128)(2,1)}, u32[]{:S(2)}, u32[]{:S(2)}) async-start(bf16[64,8,384]{2,0,1:T(8,128)(2,1)} %bitcast.122), calls=%async_computation | async-start | bytes 786432 | tf_op jit(solution)/shard_map/all_to_all | solution.py:65
  90.3 20.1 %all-to-all-start.3 = ((bf16[64,8,384]{2,0,1:T(8,128)(2,1)}), bf16[64,8,384]{2,0,1:T(8,128)(2,1)}, u32[]{:S(2)}, u32[]{:S(2)}) async-start(bf16[64,8,384]{2,0,1:T(8,128)(2,1)} %copy.79), calls=%async_computation.3 | async-start | bytes 786432 | tf_op jit(solution)/shard_map/all_to_all | solution.py:66
  96.9 55.3 %all-gather.3.cloned.1.call-start = ((), (), s32[]{:S(2)}) async-start(), calls=%async_computation.6 | async-start | bytes 3538944 | tf_op jit(solution)/shard_map/all_gather | solution.py:77
  113.6 132.1 %all-gather.5.cloned.1.call-start = ((), (), s32[]{:S(2)}) async-start(), calls=%async_computation.7 | async-start | bytes 8519680 | tf_op jit(solution)/shard_map/all_gather | solution.py:8
  152.2 3.1 %copy-start.1 = (bf16[512,3072]{1,0:T(8,128)(2,1)S(1)}, bf16[512,3072]{1,0:T(8,128)(2,1)}, u32[]{:S(2)}) copy-start(bf16[512,3072]{1,0:T(8,128)(2,1)} %all-gather.3.cloned.1.call-done) | copy-start | bytes 9437188
  159.6 0.9 copy-start.4
  166.6 25.5 %copy-start.11 = (pred[72]{0:T(512)(128)(4,1)S(1)}, pred[72]{0:T(512)(128)(4,1)}, u32[]{:S(2)}) copy-start(pred[72]{0:T(512)(128)(4,1)} %get-tuple-element.20) | copy-start | bytes 220
  192.1 3.0 %copy-start.10 = (f32[72]{0:T(128)S(1)}, f32[72]{0:T(128)}, u32[]{:S(2)}) copy-start(f32[72]{0:T(128)} %copy-done.9) | copy-start | bytes 868
  192.1 3.0 %copy-start.12 = (s32[72]{0:T(128)S(1)}, s32[72]{0:T(128)}, u32[]{:S(2)}) copy-start(s32[72]{0:T(128)} %get-tuple-element.28) | copy-start | bytes 868
  201.0 15.8 %all-to-all-start.5 = ((bf16[64,2,512]{2,1,0:T(2,128)(2,1)}), bf16[64,2,512]{2,1,0:T(2,128)(2,1)S(1)}, u32[]{:S(2)}, u32[]{:S(2)}) async-start(bf16[64,2,512]{2,1,0:T(2,128)(2,1)} %reshape.207), calls=%async_computation.5 | async-start | bytes 262144 | tf_op jit(solution)/shard_map/all_to_all | solution.py:31
Sparse Core Ops, SparseCore 0:
  113.7 38.4 all-gather.2
  157.2 88.4 all-gather.4
where the time goes:
time: 259 us; the launch traced here: 258 us
  waiting for transfers between devices  92.9 us (36%)
  starting transfers between devices  37.5 us (14%)
  local copies, waits for them, and re-layouts  35.4 us (14%)
  other arithmetic  31.5 us (12%)
  blocking collectives  23 us (9%)
  matrix products  22.8 us (9%)
  between operations  15 us (6%)
    all_gather x1, waiting for transfers between devices, local(): grad_cols = lax.all_gather(pre_grad, 'feat', axis=1, tiled=True)  38.6 us
    all_to_all x1, blocking collectives, pull_mirrors(): lax.all_to_all(outgoing, 'dom', split_axis=1, concat_axis=1, tiled=True)  23 us
    all_gather x1, waiting for transfers between devices, gathered_total(): pieces = lax.all_gather(x, axis).astype(jnp.float32)  17.9 us
    all_to_all x2, waiting for transfers between devices, push_mirrors(): lax.all_to_all(partial_value[:, masters:].astype(jnp.bfloat16), 'dom', sp...  17.1 us
    scatter-add x2, other arithmetic, push_mirrors(): return partial_value[:, :masters].at[:, targets].add(incoming, mode='drop')  16.4 us
    unnamed x39, local copies, waits for them, and re-layouts  12.5 us
    all_to_all x1, starting transfers between devices, pull_mirrors(): lax.all_to_all(outgoing, 'dom', split_axis=1, concat_axis=1, tiled=True)  11.6 us
    all_to_all x1, waiting for transfers between devices, local(): lax.all_to_all(aggregate, 'feat', split_axis=1, concat_axis=0, tiled=True)  10.7 us
  transfers between devices with their start and end apart: 7, of which 6 were waited for; matrix products, arithmetic and copies ran while one was open for 22% of the time, Pallas kernels for 0%

commit v1 on v0

v1 whole, which is shorter than its diff:
```python
import functools

import jax
import jax.numpy as jnp
from jax import lax
from jax.experimental import pallas as pl
from jax.experimental.pallas import tpu as pltpu
from jax.sharding import PartitionSpec as P

F32 = jnp.float32
BF16 = jnp.bfloat16
TILE = 128
WIDTH = 64
HALF = 8
ROWS = 3 * TILE


def nn(a, b):
    return lax.dot_general(a, b, (((1,), (0,)), ((), ())), preferred_element_type=F32)


def nt(a, b):
    return lax.dot_general(a, b, (((1,), (1,)), ((), ())), preferred_element_type=F32)


def iota(shape, dim):
    return lax.broadcasted_iota(jnp.int32, shape, dim)


def clamp(i, n):
    return jnp.minimum(jnp.maximum(i, 0), n - 1)


def tile_order(seg, src, tiles):
    wide = (tiles, TILE)
    lane, row = iota(wide, 1), iota(wide, 0)
    eye = lane == row
    pad = lane < tiles
    number = iota((tiles, 1), 0)
    key = seg * tiles + number

    def as_row(col):
        return jnp.sum(jnp.where(eye, col, 0), axis=0, keepdims=True)

    rank = jnp.sum(jnp.where(pad & (as_row(key) < key), 1, 0), axis=1, keepdims=True)
    begin = jnp.sum(jnp.where(pad & (as_row(seg) < seg), 1, 0), axis=1, keepdims=True)
    perm = rank == lane

    def sort(col):
        return jnp.sum(jnp.where(perm, col, 0), axis=0, keepdims=True)

    goes_on = jnp.where(rank == begin, 0, 1)
    last = jnp.sum(jnp.where(seg <= lane, 1, 0), axis=0, keepdims=True) - 1
    some = jnp.minimum(jnp.sum(jnp.where(seg == lane, 1, 0), axis=0, keepdims=True), 1)
    return [sort(number), sort(src), sort(goes_on), jnp.maximum(last, 0), some]


def kernel(
    n_dom, nf,
    f_ref, w_ref, tile_ref, tb_ref, tc_ref, rep_ref, cot_ref,
    out_ref, fg_ref, wg_ref,
    loc, loc2, oh, seg, snd, rcv, xbuf, meta_v, meta_s, wt, rows2, asend, pre0, pgrad, gsend, ssend, sgr,
    wsend, wpair, wown, wzs, wz, wps, wq, wfin, wall,
    meta_sem, ssems, rsems,
):
    me, mf = lax.axis_index("dom"), lax.axis_index("feat")
    ny = n_dom // 8
    chips = n_dom // 2
    my_y, core, chip = me // 8, lax.rem(me, 2), me // 2
    tiles = tile_ref.shape[0]
    width = nf * WIDTH
    nmast = 3 * nf

    barrier = pltpu.get_barrier_semaphore()

    def greet_dom(i, _):
        pl.semaphore_signal(barrier, inc=1, device_id={"dom": lax.rem(me + i, n_dom)})
        return 0

    def greet_feat(i, _):
        pl.semaphore_signal(barrier, inc=1, device_id={"feat": lax.rem(mf + i, nf)})
        return 0

    lax.fori_loop(1, n_dom, greet_dom, 0)
    lax.fori_loop(1, nf, greet_feat, 0)

    def dom_copy(src, dst, sem, peer):
        return pltpu.make_async_remote_copy(src, dst, ssems.at[sem], rsems.at[sem], device_id={"dom": peer})

    def feat_copy(src, dst, sem, peer):
        return pltpu.make_async_remote_copy(src, dst, ssems.at[sem], rsems.at[sem], device_id={"feat": peer})

    some_dom, some_feat = lax.rem(me + 1, n_dom), lax.rem(mf + 1, nf)

    for b in range(nmast):
        loc[b] = f_ref[:, b * TILE : (b + 1) * TILE]

    def build(g, _):
        rep = jnp.concatenate(
            [jnp.broadcast_to(rep_ref[0, pl.ds(g * 8 + i, 1), :], (HALF, 16)) for i in range(8)], axis=0
        ).astype(F32)
        lane, sub = iota((64, 16), 1), iota((64, 16), 0) & 7
        cols = [
            jnp.sum(jnp.where(lane == sub + 8 * h, rep, 0.0), axis=1, keepdims=True) for h in range(2)
        ]
        diff = jnp.concatenate(cols, axis=0) - iota((TILE, TILE), 1).astype(F32)
        for b in range(nmast):
            oh[pl.ds(pl.multiple_of(g * TILE, TILE), TILE), b * TILE : (b + 1) * TILE] = jnp.where(
                diff == float(b * TILE), 1.0, 0.0
            ).astype(BF16)
        return 0

    lax.fori_loop(0, ny, build, 0)

    live = iota((tiles, 1), 0) < tc_ref[0]
    source, target = tb_ref[:, 0:1], tb_ref[:, 1:2]
    table = []
    for to, frm in ((target, source), (source, target)):
        table += tile_order(jnp.where(live, to, nmast + ny), frm, tiles)
    for r, line in enumerate(table):
        meta_v[r : r + 1, :] = line
    meta_copy = pltpu.make_async_copy(meta_v, meta_s, meta_sem)
    meta_copy.start()

    r_i, c_i = iota((TILE, TILE), 0), iota((TILE, TILE), 1)
    place = ((r_i >> 3) & 7) * 16 + (r_i >> 6) * 8 + (r_i & 7)
    perm = jnp.where(place == c_i, 1.0, 0.0).astype(BF16)

    def own_zero(x):
        for d in (0, 1):
            rcv[2 * x + d, pl.ds(me, 1)] = jnp.zeros((1, HALF, TILE), BF16)

    own_zero(0)
    own_zero(1)

    pl.semaphore_wait(barrier, n_dom - 1 + nf - 1)

    def send_group(x, g, packed):
        snd[x, pl.ds(g * 8, 8)] = packed.reshape(8, HALF, TILE).astype(BF16)

        def one(i, _):
            p = g * 8 + i

            @pl.when(p != me)
            def _():
                dom_copy(snd.at[x, p], rcv.at[x, me], x, p).start()

            return 0

        lax.fori_loop(0, 8, one, 0)

    def pull(x, values):
        def body(s, _):
            g = lax.rem(my_y + s, ny)
            field = jnp.concatenate([values[b] for b in range(nmast)], axis=1)
            o = nt(oh[pl.ds(pl.multiple_of(g * TILE, TILE), TILE), :], field)
            send_group(x, g, jnp.concatenate([o[:64], o[64:]], axis=1))
            return 0

        lax.fori_loop(1, ny + 1, body, 0)

    def await_dom(x):
        dom_copy(snd.at[x, pl.ds(0, n_dom - 1)], rcv.at[x, pl.ds(0, n_dom - 1)], x, some_dom).wait_recv()

    def unpacked(x, g):
        r = rcv[x, pl.ds(g * 8, 8)].astype(F32).reshape(64, TILE)
        t = jnp.transpose(r)
        return jnp.concatenate([t[:64], t[64:]], axis=1).astype(BF16)

    def mirrors_in(x, values):
        def body(g, _):
            values[nmast + g] = nn(unpacked(x, g), perm).astype(BF16)
            return 0

        lax.fori_loop(0, ny, body, 0)

    def multiply(values, base, forward):
        def body(j, run):
            lhs = values[clamp(meta_s[base + 1, j], nmast + ny)]
            mat = tile_ref[clamp(meta_s[base, j], tiles)]
            contrib = nn(lhs, mat) if forward else nt(lhs, mat)
            run = run * meta_s[base + 2, j].astype(F32) + contrib
            seg[j] = run
            return run

        lax.fori_loop(0, tiles, body, jnp.zeros((WIDTH, TILE), F32), unroll=8)

    def partial(base, c):
        return seg[clamp(meta_s[base + 3, c], tiles)] * meta_s[base + 4, c].astype(F32)

    def push(x, base):
        def body(s, _):
            g = lax.rem(my_y + s, ny)
            o = nt(perm, partial(base, nmast + g).astype(BF16))
            send_group(x, g, jnp.concatenate([o[:64], o[64:]], axis=1))
            return 0

        lax.fori_loop(1, ny + 1, body, 0)

    def mirrors_back(x):
        def body(g, _):
            xbuf[:, pl.ds(pl.multiple_of(g * TILE, TILE), TILE)] = unpacked(x, g)
            return 0

        lax.fori_loop(0, ny, body, 0)

    def summed(base, j):
        own = jnp.concatenate([partial(base, 3 * j + r) for r in range(3)], axis=1)
        return own + nn(xbuf[...], oh[:, pl.ds(pl.multiple_of(j * ROWS, TILE), ROWS)])

    my_rows = pl.ds(pl.multiple_of(mf * WIDTH, WIDTH), WIDTH)
    S_F, S_A, S_G, S_S, S_W, S_Z, S_Q, S_L = range(4, 12)

    pull(0, loc)

    def send_features(s, _):
        j = lax.rem(mf + s, nf)
        feat_copy(
            f_ref.at[:, pl.ds(pl.multiple_of(j * ROWS, TILE), ROWS)], rows2.at[0, my_rows], S_F, j
        ).start()
        return 0

    lax.fori_loop(1, nf, send_features, 0)
    rows2[0, my_rows, :] = f_ref[:, pl.ds(pl.multiple_of(mf * ROWS, TILE), ROWS)]

    for k in range(2):
        for a in range(0, width, TILE):
            for b in range(0, width, TILE):
                wt[k, b : b + TILE, a : a + TILE] = jnp.transpose(
                    w_ref[k, a : a + TILE, b : b + TILE].astype(F32)
                ).astype(BF16)

    await_dom(0)
    mirrors_in(0, loc)
    meta_copy.wait()
    multiply(loc, 0, True)
    push(1, 0)

    def await_feat(buf, sem, peers=nf - 1):
        feat_copy(buf.at[pl.ds(0, peers)], buf.at[pl.ds(0, peers)], sem, some_feat).wait_recv()

    def await_rows(k, sem):
        got = rows2.at[k, pl.ds(0, (nf - 1) * WIDTH)]
        feat_copy(got, got, sem, some_feat).wait_recv()

    await_rows(0, S_F)

    def own_half(c, _):
        at = pl.ds(pl.multiple_of(c * TILE, TILE), TILE)
        pre0[at, :] = nn(wt[0, at, :], rows2[0])
        return 0

    lax.fori_loop(0, width // TILE, own_half, 0)

    await_dom(1)
    mirrors_back(1)

    def send_aggregate(s, _):
        j = lax.rem(mf + s, nf)
        asend[j] = summed(0, j).astype(BF16)

        @pl.when(j != mf)
        def _():
            feat_copy(asend.at[j], rows2.at[1, my_rows], S_A, j).start()

        @pl.when(j == mf)
        def _():
            rows2[1, my_rows, :] = asend[j]

        return 0

    lax.fori_loop(1, nf + 1, send_aggregate, 0)
    await_rows(1, S_A)

    def dense(c, _):
        at = pl.ds(pl.multiple_of(c * TILE, TILE), TILE)
        z = pre0[at, :] + nn(wt[1, at, :], rows2[1])
        s = jax.nn.sigmoid(z)
        out_ref[at, :] = (z * s).astype(BF16)
        slope = s * (1.0 + z * (1.0 - s))
        pgrad[at, :] = (cot_ref[at, :].astype(F32) * slope).astype(BF16)
        return 0

    lax.fori_loop(0, width // TILE, dense, 0)

    def blocked(v):
        return [v[:, r * TILE : (r + 1) * TILE].astype(BF16) for r in range(3)]

    def send_agg_grad(s, _):
        j = lax.rem(mf + s, nf)
        v = nn(w_ref[1, pl.ds(pl.multiple_of(j * WIDTH, WIDTH), WIDTH), :], pgrad[...])
        for r, part in enumerate(blocked(v)):
            gsend[j, r] = part

        @pl.when(j != mf)
        def _():
            feat_copy(gsend.at[j], loc2.at[pl.ds(3 * mf, 3)], S_G, j).start()

        @pl.when(j == mf)
        def _():
            for r in range(3):
                loc2[3 * mf + r] = gsend[j, r]

        return 0

    lax.fori_loop(1, nf + 1, send_agg_grad, 0)

    mate = me + 1 - 2 * core

    def other_terms(c, _):
        at = pl.ds(pl.multiple_of(c * TILE, TILE), TILE)
        wsend[at, :] = nt(rows2[1 - core, at, :], pgrad[...]).astype(BF16)
        return 0

    lax.fori_loop(0, width // TILE, other_terms, 0)
    dom_copy(wsend, wpair, S_W, mate).start()

    def send_self_grad(s, _):
        j = lax.rem(mf + s, nf)
        ssend[j] = nn(w_ref[0, pl.ds(pl.multiple_of(j * WIDTH, WIDTH), WIDTH), :], pgrad[...]).astype(BF16)

        @pl.when(j != mf)
        def _():
            feat_copy(ssend.at[j], sgr.at[mf], S_S, j).start()

        @pl.when(j == mf)
        def _():
            sgr[mf] = ssend[j]

        return 0

    lax.fori_loop(1, nf + 1, send_self_grad, 0)

    def own_terms(c, _):
        at = pl.ds(pl.multiple_of(c * TILE, TILE), TILE)
        wown[at, :] = nt(rows2[core, at, :], pgrad[...])
        return 0

    lax.fori_loop(0, width // TILE, own_terms, 0)

    got = loc2.at[pl.ds(0, 3 * (nf - 1))]
    feat_copy(got, got, S_G, some_feat).wait_recv()
    pull(2, loc2)

    dom_copy(wsend, wpair, S_W, mate).wait_recv()

    def send_terms(s, _):
        j = lax.rem(mf + s, nf)
        at = pl.ds(pl.multiple_of(j * WIDTH, WIDTH), WIDTH)
        wzs[j] = (wown[at, :] + wpair[at, :].astype(F32)).astype(BF16)

        @pl.when(j != mf)
        def _():
            feat_copy(wzs.at[j], wz.at[mf], S_Z, j).start()

        @pl.when(j == mf)
        def _():
            wz[mf] = wzs[j]

        return 0

    lax.fori_loop(1, nf + 1, send_terms, 0)

    await_dom(2)
    mirrors_in(2, loc2)
    multiply(loc2, 5, False)
    push(3, 5)

    await_feat(wz, S_Z)
    pr, pc = WIDTH // ny, width // 4
    total = wz[0].astype(F32)
    for j in range(1, nf):
        total = total + wz[j].astype(F32)
    for y in range(ny):
        for x in range(4):
            wps[4 * y + x] = total[y * pr : (y + 1) * pr, x * pc : (x + 1) * pc].astype(BF16)

    def send_pieces(i, _):
        p = lax.rem(chip + i, chips)
        dom_copy(wps.at[p], wq.at[chip], S_Q, 2 * p + core).start()
        return 0

    lax.fori_loop(1, chips, send_pieces, 0)
    wq[chip] = wps[chip]

    await_feat(sgr, S_S)
    await_dom(3)
    mirrors_back(3)

    def finish(j, _):
        at = pl.ds(pl.multiple_of(j * ROWS, TILE), ROWS)
        fg_ref[:, at] = (sgr[j].astype(F32) + summed(5, j)).astype(BF16)
        return 0

    dom_copy(wq.at[pl.ds(0, chips - 1)], wq.at[pl.ds(0, chips - 1)], S_Q, some_dom).wait_recv()
    whole = wq[0].astype(F32)
    for i in range(1, chips):
        whole = whole + wq[i].astype(F32)
    wfin[...] = whole.astype(BF16)
    wall[me] = whole.astype(BF16)

    def send_final(i, _):
        dom_copy(wfin, wall.at[me], S_L, lax.rem(me + i, n_dom)).start()
        return 0

    lax.fori_loop(1, n_dom, send_final, 0)

    lax.fori_loop(0, nf, finish, 0)

    dom_copy(wall.at[pl.ds(0, n_dom - 1)], wall.at[pl.ds(0, n_dom - 1)], S_L, some_dom).wait_recv()
    for d in range(n_dom):
        y, x, c = d // 8, (d // 2) % 4, d % 2
        wg_ref[c, y * pr : (y + 1) * pr, x * pc : (x + 1) * pc] = wall[d].astype(F32)

    for x in range(4):
        dom_copy(snd.at[x, pl.ds(0, n_dom - 1)], rcv.at[x, pl.ds(0, n_dom - 1)], x, some_dom).wait_send()
    for sem, buf in ((S_F, asend), (S_A, asend), (S_G, gsend), (S_S, ssend), (S_Z, wzs)):
        part = buf.at[pl.ds(0, nf - 1)]
        feat_copy(part, part, sem, some_feat).wait_send()
    dom_copy(wsend, wpair, S_W, mate).wait_send()
    dom_copy(wps.at[pl.ds(0, chips - 1)], wq.at[pl.ds(0, chips - 1)], S_Q, some_dom).wait_send()
    dom_copy(wall.at[pl.ds(0, n_dom - 1)], wall.at[pl.ds(0, n_dom - 1)], S_L, some_dom).wait_send()


def local(n_dom, nf, features, weights, tile_values, tile_blocks, tile_counts, replica, cotangent):
    width, tiles = nf * WIDTH, tile_values.shape[0]
    masters = features.shape[1]
    ny, chips = n_dom // 8, n_dom // 2
    nb = 3 * nf + ny
    piece = (WIDTH // ny, width // 4)
    vmem = pl.BlockSpec(memory_space=pltpu.VMEM)
    return pl.pallas_call(
        functools.partial(kernel, n_dom, nf),
        out_shape=(
            jax.ShapeDtypeStruct((width, ROWS), BF16),
            jax.ShapeDtypeStruct((WIDTH, masters), BF16),
            jax.ShapeDtypeStruct((2, WIDTH, width), F32),
        ),
        in_specs=[vmem, vmem, vmem, vmem, pl.BlockSpec(memory_space=pltpu.SMEM), vmem, vmem],
        out_specs=(vmem, vmem, vmem),
        scratch_shapes=[
            pltpu.VMEM((nb, WIDTH, TILE), BF16),
            pltpu.VMEM((nb, WIDTH, TILE), BF16),
            pltpu.VMEM((n_dom * 16, masters), BF16),
            pltpu.VMEM((tiles, WIDTH, TILE), F32),
            pltpu.VMEM((4, n_dom, HALF, TILE), BF16),
            pltpu.VMEM((4, n_dom, HALF, TILE), BF16),
            pltpu.VMEM((WIDTH, n_dom * 16), BF16),
            pltpu.VMEM((16, TILE), jnp.int32),
            pltpu.SMEM((16, TILE), jnp.int32),
            pltpu.VMEM((2, width, width), BF16),
            pltpu.VMEM((2, width, ROWS), BF16),
            pltpu.VMEM((nf, WIDTH, ROWS), BF16),
            pltpu.VMEM((width, ROWS), F32),
            pltpu.VMEM((width, ROWS), BF16),
            pltpu.VMEM((nf, 3, WIDTH, TILE), BF16),
            pltpu.VMEM((nf, WIDTH, ROWS), BF16),
            pltpu.VMEM((nf, WIDTH, ROWS), BF16),
            pltpu.VMEM((width, width), BF16),
            pltpu.VMEM((width, width), BF16),
            pltpu.VMEM((width, width), F32),
            pltpu.VMEM((nf, WIDTH, width), BF16),
            pltpu.VMEM((nf, WIDTH, width), BF16),
            pltpu.VMEM((chips, *piece), BF16),
            pltpu.VMEM((chips, *piece), BF16),
            pltpu.VMEM(piece, BF16),
            pltpu.VMEM((n_dom, *piece), BF16),
            pltpu.SemaphoreType.DMA,
            pltpu.SemaphoreType.DMA((12,)),
            pltpu.SemaphoreType.DMA((12,)),
        ],
        compiler_params=pltpu.CompilerParams(
            collective_id=0, has_side_effects=True, vmem_limit_bytes=48 * 2**20
        ),
    )(features, weights, tile_values, tile_blocks, tile_counts, replica, cotangent)


def solution(mesh):
    return jax.shard_map(
        functools.partial(local, mesh.shape["dom"], mesh.shape["feat"]),
        mesh=mesh,
        in_specs=(
            P("feat", "dom"),
            P(),
            P("dom", None, None),
            P("dom", None),
            P("dom"),
            P("dom", None, None),
            P(None, ("dom", "feat")),
        ),
        out_specs=(P(None, ("dom", "feat")), P("feat", "dom"), P(None, "feat", None)),
        check_vma=False,
    )
```

time: 259 us -> 106 us (0.41)
  Pallas kernels: 0 us -> 96.2 us
  waiting for transfers between devices: 92.9 us -> 0 us
  starting transfers between devices: 37.5 us -> 0 us
  other arithmetic: 31.5 us -> 0 us
  local copies, waits for them, and re-layouts: 35.4 us -> 8.62 us
  blocking collectives: 23 us -> 0 us
  matrix products: 22.8 us -> 0 us
  between operations: 15 us -> 1.3 us
    pallas_call x0 -> x1, Pallas kernels: none -> 96.2 us  [local(): pl.pallas_call(functools.partial(kernel, n_dom, nf), out_shape=(jax.Shape...]
    all_gather x2 -> x0, waiting for transfers between devices: 56.4 us -> none  [the longest x1 38.6 us: local(): grad_cols = lax.all_gather(pre_grad, 'feat', axis=1, tiled=True)]
    all_to_all x5 -> x0, starting transfers between devices: 37.2 us -> none  [the longest x1 11.6 us: pull_mirrors(): lax.all_to_all(outgoing, 'dom', split_axis=1, concat_axis=1, tiled=True)]
    all_to_all x5 -> x0, waiting for transfers between devices: 36.4 us -> none  [the longest x2 17.1 us: push_mirrors(): lax.all_to_all(partial_value[:, masters:].astype(jnp.bfloat16), 'dom', sp...]
    all_to_all x1 -> x0, blocking collectives: 23 us -> none  [pull_mirrors(): lax.all_to_all(outgoing, 'dom', split_axis=1, concat_axis=1, tiled=True)]
    dot_general x9 -> x0, matrix products: 22.8 us -> none  [the longest x2 5.31 us: spread(): jnp.einsum('ftd,tb->fbd', contrib, onehot, precision=lax.Precision.HIGHEST)]
    scatter-add x2 -> x0, other arithmetic: 16.4 us -> none  [push_mirrors(): return partial_value[:, :masters].at[:, targets].add(incoming, mode='drop')]
    gather x4 -> x0, local copies, waits for them, and re-layouts: 12.3 us -> none  [the longest x2 8.63 us: pull_mirrors(): jnp.take(values_in, slot_index, axis=1)]
  transfers between devices with their start and end apart: 7 -> 0, of which waited for: 6 -> 0; matrix products, arithmetic and copies ran while one was open for 22% -> 0% of each run, Pallas kernels for 0% -> 0%
where the time goes in v1:
time: 106 us
  Pallas kernels  96.2 us (91%)
  local copies, waits for them, and re-layouts  8.62 us (8%)
  between operations  1.3 us (1%)
    pallas_call x1, Pallas kernels, local(): pl.pallas_call(functools.partial(kernel, n_dom, nf), out_shape=(jax.Shape...  96.2 us
    unnamed x13, local copies, waits for them, and re-layouts  8.62 us

profile of v1, /device:TPU:1, one launch (start us, length us, event | category | flops | bytes accessed | tf_op | source)
XLA Modules:
  0.0 106.1 jit_solution(11007642552384660139)
XLA Ops:
  1.3 0.8 copy.11.rep_ref
  2.1 0.8 copy.10.tb_ref
  2.8 0.0 copy-start
  2.8 1.7 %copy-done = bf16[72,128,128]{2,1,0:T(8,128)(2,1)S(1)} copy-done((bf16[72,128,128]{2,1,0:T(8,128)(2,1)S(1)}, bf16[72,128,128]{2,1,0:T(8,128)(2,1)}, u32[]{:S(2)}) %copy-start) | copy-done | bytes 2359320
  4.5 0.0 copy-start.1
  4.5 1.2 %copy-done.1 = bf16[2,512,512]{2,1,0:T(8,128)(2,1)S(1)} copy-done((bf16[2,512,512]{2,1,0:T(8,128)(2,1)S(1)}, bf16[2,512,512]{2,1,0:T(8,128)(2,1)}, u32[]{:S(2)}) %copy-start.1) | copy-done | bytes 1048600
  5.7 0.0 copy-start.2
  5.7 1.0 copy-done.2
  6.7 0.0 copy-start.3
  6.7 1.0 copy-done.3
  7.7 96.2 %shard_map.94 = (bf16[512,384]{1,0:T(8,128)(2,1)S(1)}, bf16[64,3072]{1,0:T(8,128)(2,1)S(1)}, f32[2,64,512]{2,1,0:T(8,128)S(1)}) custom-call(bf16[64,3072]{1,0:T(8,128)(2,1)S(1)} %copy-done.2, bf16[2,512,512]{2,1,0:T(8,128)(2,1)S(1)} %copy-done.1, bf16[72,128,128]{2,1,0:T(8,128)(2,1)S(1)} %copy-done, s32[72,2]{1,0:T(8,128)S(1)} %copy.10.tb_ref, ...), custom_call_target="tpu_custom_call" | custom-call | tf_op jit(solution)/shard_map/pallas_call | solution.py:432
  103.9 0.7 copy.16
  104.7 0.7 copy.17
  105.4 0.7 copy.18
Async XLA Ops:
  2.8 1.7 %copy-start = (bf16[72,128,128]{2,1,0:T(8,128)(2,1)S(1)}, bf16[72,128,128]{2,1,0:T(8,128)(2,1)}, u32[]{:S(2)}) copy-start(bf16[72,128,128]{2,1,0:T(8,128)(2,1)} %tile_ref.1) | copy-start | bytes 7077892
  4.5 1.2 %copy-start.1 = (bf16[2,512,512]{2,1,0:T(8,128)(2,1)S(1)}, bf16[2,512,512]{2,1,0:T(8,128)(2,1)}, u32[]{:S(2)}) copy-start(bf16[2,512,512]{2,1,0:T(8,128)(2,1)} %w_ref.1) | copy-start | bytes 3145732
  5.7 1.0 copy-start.2
  6.7 1.0 copy-start.3

commit v2 on v1

v2 whole, which is shorter than its diff:
```python
import functools

import jax
import jax.numpy as jnp
from jax import lax
from jax.experimental import pallas as pl
from jax.experimental.pallas import tpu as pltpu
from jax.sharding import PartitionSpec as P

F32 = jnp.float32
BF16 = jnp.bfloat16
TILE = 128
WIDTH = 64
HALF = 8
ROWS = 3 * TILE


def nn(a, b):
    return lax.dot_general(a, b, (((1,), (0,)), ((), ())), preferred_element_type=F32)


def nt(a, b):
    return lax.dot_general(a, b, (((1,), (1,)), ((), ())), preferred_element_type=F32)


def iota(shape, dim):
    return lax.broadcasted_iota(jnp.int32, shape, dim)


def clamp(i, n):
    return jnp.minimum(jnp.maximum(i, 0), n - 1)


def tile_order(seg, src, tiles):
    lane, row = iota((tiles, TILE), 1), iota((tiles, TILE), 0)
    eye = iota((tiles, tiles), 0) == iota((tiles, tiles), 1)
    number = iota((1, tiles), 1)

    def as_col(line):
        return jnp.sum(jnp.where(eye, line, 0), axis=1, keepdims=True)

    key = seg * tiles + number
    seg_col, key_col = as_col(seg), as_col(key)
    rank = jnp.sum(jnp.where(key < key_col, 1, 0), axis=1, keepdims=True)
    begin = jnp.sum(jnp.where(seg < seg_col, 1, 0), axis=1, keepdims=True)
    perm = rank == lane

    def sort(col):
        return jnp.sum(jnp.where(perm, col, 0), axis=0, keepdims=True)

    goes_on = jnp.where(rank == begin, 0, 1)
    last = jnp.sum(jnp.where(seg_col <= lane, 1, 0), axis=0, keepdims=True) - 1
    some = jnp.minimum(jnp.sum(jnp.where(seg_col == lane, 1, 0), axis=0, keepdims=True), 1)
    return [sort(row[:, 0:1]), sort(as_col(src)), sort(goes_on), jnp.maximum(last, 0), some]


def kernel(
    n_dom, nf,
    f_in, w_in, tile_in, tb_in, tc_ref, rep_in, cot_in,
    out_ref, fg_ref, wg_ref,
    f_ref, w_ref, tile_ref, tb_ref, rep_ref, cot_ref,
    loc, loc2, oh, seg, snd, rcv, xbuf, acc, meta_v, meta_s, wt, rows, asend, pre0, pgrad, gsend, ssend, sgr,
    wsend, wpair, wown, wzs, wz, wps, wq, wfin, wall,
    meta_sem, load_sems, ssems, rsems,
):
    me, mf = lax.axis_index("dom"), lax.axis_index("feat")
    ny = n_dom // 8
    chips = n_dom // 2
    my_y, core, chip = me // 8, lax.rem(me, 2), me // 2
    tiles = tile_in.shape[0]
    width = nf * WIDTH
    nmast = 3 * nf
    span = nf * TILE

    loads = [
        pltpu.make_async_copy(src, dst, load_sems.at[i])
        for i, (src, dst) in enumerate(
            (
                (rep_in, rep_ref),
                (f_in, f_ref),
                (tb_in, tb_ref),
                (w_in, w_ref),
                (tile_in, tile_ref),
                (cot_in, cot_ref),
            )
        )
    ]
    for load in loads:
        load.start()

    barrier = pltpu.get_barrier_semaphore()

    def greet_dom(i, _):
        pl.semaphore_signal(barrier, inc=1, device_id={"dom": lax.rem(me + i, n_dom)})
        return 0

    def greet_feat(i, _):
        pl.semaphore_signal(barrier, inc=1, device_id={"feat": lax.rem(mf + i, nf)})
        return 0

    lax.fori_loop(1, n_dom, greet_dom, 0)
    lax.fori_loop(1, nf, greet_feat, 0)

    def dom_copy(src, dst, sem, peer):
        return pltpu.make_async_remote_copy(src, dst, ssems.at[sem], rsems.at[sem], device_id={"dom": peer})

    def feat_copy(src, dst, sem, peer):
        return pltpu.make_async_remote_copy(src, dst, ssems.at[sem], rsems.at[sem], device_id={"feat": peer})

    some_dom, some_feat = lax.rem(me + 1, n_dom), lax.rem(mf + 1, nf)
    my_rows = pl.ds(pl.multiple_of(mf * WIDTH, WIDTH), WIDTH)
    S_F, S_A, S_G, S_S, S_W, S_Z, S_Q, S_L = 4, 5, 8, 11, 12, 13, 14, 15

    def far_first(start, n, step):
        def body(s, _):
            away = n // 2 + ((s + 1) // 2) * (1 - 2 * lax.rem(s, 2))
            step(lax.rem(start + away, n))
            return 0

        lax.fori_loop(0, n, body, 0)

    def rows_of(c):
        return pl.ds(pl.multiple_of(c * TILE, TILE), TILE)

    loads[0].wait()
    loads[1].wait()
    for b in range(nmast):
        loc[b] = f_ref[:, b * TILE : (b + 1) * TILE]

    def build(g, _):
        wide = (8 * HALF, n_dom)
        mine = iota(wide, 1) == g * 8 + (iota(wide, 0) >> 3)
        cols = []
        for h in range(2):
            slots = rep_ref[0, h * HALF : (h + 1) * HALF, :].astype(F32)
            slots = jnp.concatenate([slots] * 8, axis=0)
            cols.append(jnp.sum(jnp.where(mine, slots, 0.0), axis=1, keepdims=True))
        diff = jnp.concatenate(cols, axis=0) - iota((TILE, TILE), 1).astype(F32)
        for r in range(3):
            for f in range(nf):
                at = r * span + f * TILE
                oh[rows_of(g), at : at + TILE] = jnp.where(
                    diff == float((3 * f + r) * TILE), 1.0, 0.0
                ).astype(BF16)
        return 0

    lax.fori_loop(0, ny, build, 0)

    for x in range(4):
        rcv[x, pl.ds(me, 1)] = jnp.zeros((1, HALF, TILE), BF16)

    def chunk(values, r):
        return jnp.concatenate([values[3 * f + r] for f in range(nf)], axis=1)

    def pack(x, g, o):
        side_by_side = jnp.concatenate([o[:64], o[64:]], axis=1)
        snd[x, pl.ds(g * 8, 8)] = side_by_side.reshape(8, HALF, TILE).astype(BF16)

    def send_group(x, g):
        def one(i, _):
            p = g * 8 + i

            @pl.when(p != me)
            def _():
                dom_copy(snd.at[x, p], rcv.at[x, me], x, p).start()

            return 0

        lax.fori_loop(0, 8, one, 0)

    def first_pull(g, _):
        field = jnp.concatenate([chunk(loc, r) for r in range(3)], axis=1)
        pack(0, g, nt(oh[rows_of(g), :], field))
        return 0

    lax.fori_loop(0, ny, first_pull, 0)

    loads[2].wait()
    live = iota((1, tiles), 1) < tc_ref[0]
    source, target = tb_ref[0:1, :], tb_ref[1:2, :]
    table = []
    for to, frm in ((target, source), (source, target)):
        table += tile_order(jnp.where(live, to, nmast + ny), frm, tiles)
    for r, line in enumerate(table):
        meta_v[r : r + 1, :] = line
    meta_copy = pltpu.make_async_copy(meta_v, meta_s, meta_sem)
    meta_copy.start()

    r_i, c_i = iota((TILE, TILE), 0), iota((TILE, TILE), 1)
    place = ((r_i >> 3) & 7) * 16 + (r_i >> 6) * 8 + (r_i & 7)
    perm = jnp.where(place == c_i, 1.0, 0.0).astype(BF16)

    loads[3].wait()
    for k in range(2):
        for a in range(0, width, TILE):
            for b in range(0, width, TILE):
                wt[k, b : b + TILE, a : a + TILE] = jnp.transpose(
                    w_ref[k, a : a + TILE, b : b + TILE].astype(F32)
                ).astype(BF16)
    loads[4].wait()
    loads[5].wait()
    meta_copy.wait()

    pl.semaphore_wait(barrier, n_dom - 1 + nf - 1)

    far_first(my_y, ny, lambda g: send_group(0, g))

    def send_features(j):
        theirs = loc.at[pl.ds(3 * j, 3)]

        @pl.when(j != mf)
        def _():
            feat_copy(theirs, rows.at[0, :, my_rows, :], S_F, j).start()

    far_first(mf, nf, send_features)
    for r in range(3):
        rows[0, r, my_rows, :] = loc[3 * mf + r]

    def await_dom(x):
        dom_copy(snd.at[x, pl.ds(0, n_dom - 1)], rcv.at[x, pl.ds(0, n_dom - 1)], x, some_dom).wait_recv()

    def await_blocks(buf, sem, n):
        feat_copy(buf.at[pl.ds(0, n)], buf.at[pl.ds(0, n)], sem, some_feat).wait_recv()

    def unpacked(x, g):
        t = jnp.transpose(rcv[x, pl.ds(g * 8, 8)].astype(F32).reshape(64, TILE))
        return jnp.concatenate([t[:64], t[64:]], axis=1).astype(BF16)

    def mirrors_in(x, values):
        def body(g, _):
            values[nmast + g] = nn(unpacked(x, g), perm).astype(BF16)
            return 0

        lax.fori_loop(0, ny, body, 0)

    def multiply(values, base, forward, low, high, start):
        def body(j, run):
            lhs = values[clamp(meta_s[base + 1, j], nmast + ny)]
            mat = tile_ref[clamp(meta_s[base, j], tiles)]
            contrib = nn(lhs, mat) if forward else nt(lhs, mat)
            run = run * meta_s[base + 2, j].astype(F32) + contrib
            seg[j] = run
            return run

        return lax.fori_loop(low, high, body, start, unroll=12)

    def partial(base, c):
        return seg[clamp(meta_s[base + 3, c], tiles)] * meta_s[base + 4, c].astype(F32)

    def push(x, base):
        def body(g):
            pack(x, g, nt(perm, partial(base, nmast + g).astype(BF16)))
            send_group(x, g)

        far_first(my_y, ny, body)

    def mirrors_back(x):
        def body(g, _):
            xbuf[:, rows_of(g)] = unpacked(x, g)
            return 0

        lax.fori_loop(0, ny, body, 0)

    def summed(base, j, r):
        at = pl.ds(pl.multiple_of(r * span + j * TILE, TILE), TILE)
        return partial(base, 3 * j + r) + nn(xbuf[...], oh[:, at])

    nothing = jnp.zeros((WIDTH, TILE), F32)
    await_dom(0)
    mirrors_in(0, loc)
    multiply(loc, 0, True, 0, tiles, nothing)
    push(1, 0)

    await_blocks(loc, S_F, 3 * (nf - 1))

    def own_half(c, _):
        for r in range(3):
            pre0[r, rows_of(c), :] = nn(wt[0, rows_of(c), :], rows[0, r])
        return 0

    lax.fori_loop(0, width // TILE, own_half, 0)

    await_dom(1)
    mirrors_back(1)

    for r in range(3):

        def send_aggregate(j, r=r):
            asend[r, j] = summed(0, j, r).astype(BF16)

            @pl.when(j != mf)
            def _():
                feat_copy(asend.at[r, j], rows.at[1, r, my_rows, :], S_A + r, j).start()

            @pl.when(j == mf)
            def _():
                rows[1, r, my_rows, :] = asend[r, j]

        far_first(mf, nf, send_aggregate)

    for r in range(3):
        await_blocks(asend.at[r], S_A + r, nf - 1)

        def dense(c, _, r=r):
            at = rows_of(c)
            z = pre0[r, at, :] + nn(wt[1, at, :], rows[1, r])
            s = jax.nn.sigmoid(z)
            out_ref[at, r * TILE : (r + 1) * TILE] = (z * s).astype(BF16)
            slope = s * (1.0 + z * (1.0 - s))
            cot = cot_ref[at, r * TILE : (r + 1) * TILE].astype(F32)
            pgrad[r, at, :] = (cot * slope).astype(BF16)
            return 0

        lax.fori_loop(0, width // TILE, dense, 0)

        def agg_grad(c, _, r=r):
            v = nn(w_ref[1, rows_of(c), :], pgrad[r]).astype(BF16)
            gsend[r, 2 * c] = v[:WIDTH]
            gsend[r, 2 * c + 1] = v[WIDTH:]
            return 0

        lax.fori_loop(0, width // TILE, agg_grad, 0)

        def send_agg_grad(j, r=r):
            @pl.when(j != mf)
            def _():
                feat_copy(gsend.at[r, j], loc2.at[3 * mf + r], S_G + r, j).start()

            @pl.when(j == mf)
            def _():
                loc2[3 * mf + r] = gsend[r, j]

        far_first(mf, nf, send_agg_grad)

    mate = me + 1 - 2 * core

    def terms(k, c):
        mine = jnp.concatenate([rows[k, r, rows_of(c), :] for r in range(3)], axis=1)
        return nt(mine, jnp.concatenate([pgrad[r] for r in range(3)], axis=1))

    def other_terms(c, _):
        wsend[rows_of(c), :] = terms(1 - core, c).astype(BF16)
        return 0

    lax.fori_loop(0, width // TILE, other_terms, 0)
    dom_copy(wsend, wpair, S_W, mate).start()

    def own_terms(c, _):
        wown[rows_of(c), :] = terms(core, c)
        return 0

    lax.fori_loop(0, width // TILE, own_terms, 0)

    def gathered(g, r):
        return nt(oh[rows_of(g), r * span : (r + 1) * span], chunk(loc2, r))

    def pull_first(g, _):
        acc[g] = gathered(g, 0)
        return 0

    def pull_second(g, _):
        acc[g] = acc[g] + gathered(g, 1)
        return 0

    def pull_last(g):
        pack(2, g, acc[g] + gathered(g, 2))
        send_group(2, g)

    await_blocks(loc2, S_G, nf - 1)
    lax.fori_loop(0, ny, pull_first, 0)

    dom_copy(wsend, wpair, S_W, mate).wait_recv()

    def send_terms(j):
        at = pl.ds(pl.multiple_of(j * WIDTH, WIDTH), WIDTH)
        wzs[j] = (wown[at, :] + wpair[at, :].astype(F32)).astype(BF16)

        @pl.when(j != mf)
        def _():
            feat_copy(wzs.at[j], wz.at[mf], S_Z, j).start()

        @pl.when(j == mf)
        def _():
            wz[mf] = wzs[j]

    far_first(mf, nf, send_terms)

    await_blocks(loc2, S_G + 1, nf - 1)
    lax.fori_loop(0, ny, pull_second, 0)
    await_blocks(loc2, S_G + 2, nf - 1)
    far_first(my_y, ny, pull_last)

    def send_self_grad(j):
        w = w_ref[0, pl.ds(pl.multiple_of(j * WIDTH, WIDTH), WIDTH), :]
        for r in range(3):
            ssend[j, r] = nn(w, pgrad[r]).astype(BF16)

        @pl.when(j != mf)
        def _():
            feat_copy(ssend.at[j], sgr.at[mf], S_S, j).start()

        @pl.when(j == mf)
        def _():
            sgr[mf] = ssend[j]

    far_first(mf, nf, send_self_grad)

    await_dom(2)
    mirrors_in(2, loc2)
    run = multiply(loc2, 5, False, 0, tiles // 2, nothing)

    await_blocks(wz, S_Z, nf - 1)
    pr, pc = WIDTH // ny, width // 4
    total = wz[0].astype(F32)
    for j in range(1, nf):
        total = total + wz[j].astype(F32)
    for y in range(ny):
        for x in range(4):
            wps[4 * y + x] = total[y * pr : (y + 1) * pr, x * pc : (x + 1) * pc].astype(BF16)

    def send_pieces(i, _):
        p = lax.rem(chip + i, chips)
        dom_copy(wps.at[p], wq.at[chip], S_Q, 2 * p + core).start()
        return 0

    lax.fori_loop(1, chips, send_pieces, 0)
    wq[chip] = wps[chip]

    multiply(loc2, 5, False, tiles // 2, tiles, run)
    push(3, 5)

    dom_copy(wq.at[pl.ds(0, chips - 1)], wq.at[pl.ds(0, chips - 1)], S_Q, some_dom).wait_recv()
    whole = wq[0].astype(F32)
    for i in range(1, chips):
        whole = whole + wq[i].astype(F32)
    wfin[...] = whole.astype(BF16)
    wall[me] = whole.astype(BF16)

    def send_final(i, _):
        dom_copy(wfin, wall.at[me], S_L, lax.rem(me + i, n_dom)).start()
        return 0

    lax.fori_loop(1, n_dom, send_final, 0)

    await_blocks(sgr, S_S, nf - 1)
    await_dom(3)
    mirrors_back(3)

    def finish(j, _):
        for r in range(3):
            at = pl.ds(pl.multiple_of(j * ROWS + r * TILE, TILE), TILE)
            fg_ref[:, at] = (sgr[j, r].astype(F32) + summed(5, j, r)).astype(BF16)
        return 0

    lax.fori_loop(0, nf, finish, 0)

    dom_copy(wall.at[pl.ds(0, n_dom - 1)], wall.at[pl.ds(0, n_dom - 1)], S_L, some_dom).wait_recv()
    for d in range(n_dom):
        y, x, c = d // 8, (d // 2) % 4, d % 2
        wg_ref[c, y * pr : (y + 1) * pr, x * pc : (x + 1) * pc] = wall[d].astype(F32)

    for x in range(4):
        dom_copy(snd.at[x, pl.ds(0, n_dom - 1)], rcv.at[x, pl.ds(0, n_dom - 1)], x, some_dom).wait_send()

    def drain(buf, sem):
        part = buf.at[pl.ds(0, nf - 1)]
        feat_copy(part, part, sem, some_feat).wait_send()

    for sem, buf in ((S_F, ssend), (S_S, ssend), (S_Z, wzs)):
        drain(buf, sem)
    for r in range(3):
        drain(asend.at[r], S_A + r)
        drain(gsend.at[r], S_G + r)
    dom_copy(wsend, wpair, S_W, mate).wait_send()
    dom_copy(wps.at[pl.ds(0, chips - 1)], wq.at[pl.ds(0, chips - 1)], S_Q, some_dom).wait_send()
    dom_copy(wall.at[pl.ds(0, n_dom - 1)], wall.at[pl.ds(0, n_dom - 1)], S_L, some_dom).wait_send()


def pinned(x):
    return pltpu.with_memory_space_constraint(x, pltpu.HBM)


def local(n_dom, nf, features, weights, tile_values, tile_blocks, tile_counts, replica, cotangent):
    width, tiles = nf * WIDTH, tile_values.shape[0]
    masters = features.shape[1]
    ny, chips = n_dom // 8, n_dom // 2
    nb = 3 * nf + ny
    piece = (WIDTH // ny, width // 4)
    vmem = pl.BlockSpec(memory_space=pltpu.VMEM)
    hbm = pl.BlockSpec(memory_space=pltpu.HBM)
    return pl.pallas_call(
        functools.partial(kernel, n_dom, nf),
        out_shape=(
            jax.ShapeDtypeStruct((width, ROWS), BF16),
            jax.ShapeDtypeStruct((WIDTH, masters), BF16),
            jax.ShapeDtypeStruct((2, WIDTH, width), F32),
        ),
        in_specs=[hbm, hbm, hbm, hbm, pl.BlockSpec(memory_space=pltpu.SMEM), hbm, hbm],
        out_specs=(vmem, vmem, vmem),
        scratch_shapes=[
            pltpu.VMEM((WIDTH, masters), BF16),
            pltpu.VMEM((2, width, width), BF16),
            pltpu.VMEM((tiles, TILE, TILE), BF16),
            pltpu.VMEM((2, tiles), jnp.int32),
            pltpu.VMEM((1, 16, n_dom), jnp.int32),
            pltpu.VMEM((width, ROWS), BF16),
            pltpu.VMEM((nb, WIDTH, TILE), BF16),
            pltpu.VMEM((nb, WIDTH, TILE), BF16),
            pltpu.VMEM((n_dom * 16, masters), BF16),
            pltpu.VMEM((tiles, WIDTH, TILE), F32),
            pltpu.VMEM((4, n_dom, HALF, TILE), BF16),
            pltpu.VMEM((4, n_dom, HALF, TILE), BF16),
            pltpu.VMEM((WIDTH, n_dom * 16), BF16),
            pltpu.VMEM((ny, TILE, WIDTH), F32),
            pltpu.VMEM((16, TILE), jnp.int32),
            pltpu.SMEM((16, TILE), jnp.int32),
            pltpu.VMEM((2, width, width), BF16),
            pltpu.VMEM((2, 3, width, TILE), BF16),
            pltpu.VMEM((3, nf, WIDTH, TILE), BF16),
            pltpu.VMEM((3, width, TILE), F32),
            pltpu.VMEM((3, width, TILE), BF16),
            pltpu.VMEM((3, nf, WIDTH, TILE), BF16),
            pltpu.VMEM((nf, 3, WIDTH, TILE), BF16),
            pltpu.VMEM((nf, 3, WIDTH, TILE), BF16),
            pltpu.VMEM((width, width), BF16),
            pltpu.VMEM((width, width), BF16),
            pltpu.VMEM((width, width), F32),
            pltpu.VMEM((nf, WIDTH, width), BF16),
            pltpu.VMEM((nf, WIDTH, width), BF16),
            pltpu.VMEM((chips, *piece), BF16),
            pltpu.VMEM((chips, *piece), BF16),
            pltpu.VMEM(piece, BF16),
            pltpu.VMEM((n_dom, *piece), BF16),
            pltpu.SemaphoreType.DMA,
            pltpu.SemaphoreType.DMA((6,)),
            pltpu.SemaphoreType.DMA((16,)),
            pltpu.SemaphoreType.DMA((16,)),
        ],
        compiler_params=pltpu.CompilerParams(
            collective_id=0, has_side_effects=True, vmem_limit_bytes=48 * 2**20
        ),
    )(
        pinned(features),
        pinned(weights),
        pinned(tile_values),
        pinned(tile_blocks.T),
        tile_counts,
        pinned(jnp.swapaxes(replica, 1, 2)),
        pinned(cotangent),
    )


def solution(mesh):
    return jax.shard_map(
        functools.partial(local, mesh.shape["dom"], mesh.shape["feat"]),
        mesh=mesh,
        in_specs=(
            P("feat", "dom"),
            P(),
            P("dom", None, None),
            P("dom", None),
            P("dom"),
            P("dom", None, None),
            P(None, ("dom", "feat")),
        ),
        out_specs=(P(None, ("dom", "feat")), P("feat", "dom"), P(None, "feat", None)),
        check_vma=False,
    )
```

time: 106 us -> 89.2 us (0.84)
  Pallas kernels: 96.2 us -> 85.6 us
  local copies, waits for them, and re-layouts: 8.62 us -> 2.2 us
    pallas_call x1, Pallas kernels: 96.2 us -> 85.6 us  [local(): pl.pallas_call(functools.partial(kernel, n_dom, nf), out_shape=(jax.Shape...]
    unnamed x13 -> x3, local copies, waits for them, and re-layouts: 8.62 us -> 2.2 us
where the time goes in v2:
time: 89.2 us; the launch traced here: 89.1 us
  Pallas kernels  85.6 us (96%)
  local copies, waits for them, and re-layouts  2.2 us (2%)
  between operations  1.29 us (1%)
    pallas_call x1, Pallas kernels, local(): pl.pallas_call(functools.partial(kernel, n_dom, nf), out_shape=(jax.Shape...  85.6 us
    unnamed x3, local copies, waits for them, and re-layouts  2.2 us

profile of v2, /device:TPU:1, one launch (start us, length us, event | category | flops | bytes accessed | tf_op | source)
XLA Modules:
  0.0 89.1 jit_solution(1924326321986614523)
XLA Ops:
  1.3 85.6 %shard_map.94 = (bf16[512,384]{1,0:T(8,128)(2,1)S(1)}, bf16[64,3072]{1,0:T(8,128)(2,1)S(1)}, f32[2,64,512]{2,1,0:T(8,128)S(1)}) custom-call(bf16[64,3072]{1,0:T(8,128)(2,1)} %f_in.1, bf16[2,512,512]{2,1,0:T(8,128)(2,1)} %w_in.1, bf16[72,128,128]{2,1,0:T(8,128)(2,1)} %tile_in.1, s32[2,72]{1,0:T(2,128)} %bitcast.3, s32[1]{0:T(128)S(6)} %copy.13.tc_ref, ...), custom_call_target="tpu_custom_call" | custom-call | tf_op jit(solution)/shard_map/pallas_call | solution.py:491
  86.9 0.7 copy.14
  87.7 0.7 copy.15
  88.4 0.7 copy.16

commit v3 on v2

--- a/solution.py
+++ b/solution.py
@@ -231,7 +231,7 @@
             values[nmast + g] = nn(unpacked(x, g), perm).astype(BF16)
             return 0
 
-        lax.fori_loop(0, ny, body, 0)
+        lax.fori_loop(0, ny, body, 0, unroll=True)
 
     def multiply(values, base, forward, low, high, start):
         def body(j, run):
@@ -242,28 +242,26 @@
             seg[j] = run
             return run
 
-        return lax.fori_loop(low, high, body, start, unroll=12)
+        return lax.fori_loop(low, high, body, start, unroll=18)
 
     def partial(base, c):
         return seg[clamp(meta_s[base + 3, c], tiles)] * meta_s[base + 4, c].astype(F32)
 
     def push(x, base):
-        def body(g):
+        for g in range(ny):
             pack(x, g, nt(perm, partial(base, nmast + g).astype(BF16)))
-            send_group(x, g)
-
-        far_first(my_y, ny, body)
+        far_first(my_y, ny, lambda g: send_group(x, g))
 
     def mirrors_back(x):
         def body(g, _):
             xbuf[:, rows_of(g)] = unpacked(x, g)
             return 0
 
-        lax.fori_loop(0, ny, body, 0)
-
-    def summed(base, j, r):
-        at = pl.ds(pl.multiple_of(r * span + j * TILE, TILE), TILE)
-        return partial(base, 3 * j + r) + nn(xbuf[...], oh[:, at])
+        lax.fori_loop(0, ny, body, 0, unroll=True)
+
+    def summed(base, r):
+        back = nn(xbuf[...], oh[:, r * span : (r + 1) * span])
+        return [partial(base, 3 * f + r) + back[:, f * TILE : (f + 1) * TILE] for f in range(nf)]
 
     nothing = jnp.zeros((WIDTH, TILE), F32)
     await_dom(0)
@@ -285,41 +283,33 @@
 
     for r in range(3):
 
+        for f, block in enumerate(summed(0, r)):
+            asend[r, f] = block.astype(BF16)
+
         def send_aggregate(j, r=r):
-            asend[r, j] = summed(0, j, r).astype(BF16)
-
             @pl.when(j != mf)
             def _():
                 feat_copy(asend.at[r, j], rows.at[1, r, my_rows, :], S_A + r, j).start()
 
-            @pl.when(j == mf)
-            def _():
-                rows[1, r, my_rows, :] = asend[r, j]
-
         far_first(mf, nf, send_aggregate)
+        rows[1, r, my_rows, :] = asend[r, mf]
 
     for r in range(3):
         await_blocks(asend.at[r], S_A + r, nf - 1)
 
-        def dense(c, _, r=r):
-            at = rows_of(c)
+        cols = slice(r * TILE, (r + 1) * TILE)
+        for c in range(width // TILE):
+            at = slice(c * TILE, (c + 1) * TILE)
             z = pre0[r, at, :] + nn(wt[1, at, :], rows[1, r])
             s = jax.nn.sigmoid(z)
-            out_ref[at, r * TILE : (r + 1) * TILE] = (z * s).astype(BF16)
+            out_ref[at, cols] = (z * s).astype(BF16)
             slope = s * (1.0 + z * (1.0 - s))
-            cot = cot_ref[at, r * TILE : (r + 1) * TILE].astype(F32)
-            pgrad[r, at, :] = (cot * slope).astype(BF16)
-            return 0
-
-        lax.fori_loop(0, width // TILE, dense, 0)
-
-        def agg_grad(c, _, r=r):
-            v = nn(w_ref[1, rows_of(c), :], pgrad[r]).astype(BF16)
+            pgrad[r, at, :] = (cot_ref[at, cols].astype(F32) * slope).astype(BF16)
+
+        for c in range(width // TILE):
+            v = nn(w_ref[1, c * TILE : (c + 1) * TILE, :], pgrad[r]).astype(BF16)
             gsend[r, 2 * c] = v[:WIDTH]
             gsend[r, 2 * c + 1] = v[WIDTH:]
-            return 0
-
-        lax.fori_loop(0, width // TILE, agg_grad, 0)
 
         def send_agg_grad(j, r=r):
             @pl.when(j != mf)
@@ -342,14 +332,14 @@
         wsend[rows_of(c), :] = terms(1 - core, c).astype(BF16)
         return 0
 
-    lax.fori_loop(0, width // TILE, other_terms, 0)
+    lax.fori_loop(0, width // TILE, other_terms, 0, unroll=True)
     dom_copy(wsend, wpair, S_W, mate).start()
 
     def own_terms(c, _):
         wown[rows_of(c), :] = terms(core, c)
         return 0
 
-    lax.fori_loop(0, width // TILE, own_terms, 0)
+    lax.fori_loop(0, width // TILE, own_terms, 0, unroll=True)
 
     def gathered(g, r):
         return nt(oh[rows_of(g), r * span : (r + 1) * span], chunk(loc2, r))
@@ -367,7 +357,7 @@
         send_group(2, g)
 
     await_blocks(loc2, S_G, nf - 1)
-    lax.fori_loop(0, ny, pull_first, 0)
+    lax.fori_loop(0, ny, pull_first, 0, unroll=True)
 
     dom_copy(wsend, wpair, S_W, mate).wait_recv()
 
@@ -386,7 +376,7 @@
     far_first(mf, nf, send_terms)
 
     await_blocks(loc2, S_G + 1, nf - 1)
-    lax.fori_loop(0, ny, pull_second, 0)
+    lax.fori_loop(0, ny, pull_second, 0, unroll=True)
     await_blocks(loc2, S_G + 2, nf - 1)
     far_first(my_y, ny, pull_last)
 
@@ -446,13 +436,10 @@
     await_dom(3)
     mirrors_back(3)
 
-    def finish(j, _):
-        for r in range(3):
-            at = pl.ds(pl.multiple_of(j * ROWS + r * TILE, TILE), TILE)
-            fg_ref[:, at] = (sgr[j, r].astype(F32) + summed(5, j, r)).astype(BF16)
-        return 0
-
-    lax.fori_loop(0, nf, finish, 0)
+    for r in range(3):
+        for f, block in enumerate(summed(5, r)):
+            at = (3 * f + r) * TILE
+            fg_ref[:, at : at + TILE] = (sgr[f, r].astype(F32) + block).astype(BF16)
 
     dom_copy(wall.at[pl.ds(0, n_dom - 1)], wall.at[pl.ds(0, n_dom - 1)], S_L, some_dom).wait_recv()
     for d in range(n_dom):

time: 89.2 us -> 86.3 us (0.967)
  Pallas kernels: 85.6 us -> 82.7 us
    pallas_call x1, Pallas kernels: 85.6 us -> 82.7 us  [local(): pl.pallas_call(functools.partial(kernel, n_dom, nf), out_shape=(jax.Shape...]
where the time goes in v3:
time: 86.3 us; the launch traced here: 86.2 us
  Pallas kernels  82.7 us (96%)
  local copies, waits for them, and re-layouts  2.2 us (3%)
  between operations  1.29 us (1%)
    pallas_call x1, Pallas kernels, local(): pl.pallas_call(functools.partial(kernel, n_dom, nf), out_shape=(jax.Shape...  82.7 us
    unnamed x3, local copies, waits for them, and re-layouts  2.2 us

profile of v3, /device:TPU:1, one launch (start us, length us, event | category | flops | bytes accessed | tf_op | source)
XLA Modules:
  0.0 86.2 jit_solution(15485576792281474978)
XLA Ops:
  1.3 82.7 %shard_map.94 = (bf16[512,384]{1,0:T(8,128)(2,1)S(1)}, bf16[64,3072]{1,0:T(8,128)(2,1)S(1)}, f32[2,64,512]{2,1,0:T(8,128)S(1)}) custom-call(bf16[64,3072]{1,0:T(8,128)(2,1)} %f_in.1, bf16[2,512,512]{2,1,0:T(8,128)(2,1)} %w_in.1, bf16[72,128,128]{2,1,0:T(8,128)(2,1)} %tile_in.1, s32[2,72]{1,0:T(2,128)} %bitcast.3, s32[1]{0:T(128)S(6)} %copy.13.tc_ref, ...), custom_call_target="tpu_custom_call" | custom-call | tf_op jit(solution)/shard_map/pallas_call | solution.py:478
  84.0 0.7 copy.14
  84.7 0.7 copy.15
  85.5 0.7 copy.16

commit v4 on v3

--- a/solution.py
+++ b/solution.py
@@ -341,6 +341,22 @@
 
     lax.fori_loop(0, width // TILE, own_terms, 0, unroll=True)
 
+    dom_copy(wsend, wpair, S_W, mate).wait_recv()
+
+    def send_terms(j):
+        at = pl.ds(pl.multiple_of(j * WIDTH, WIDTH), WIDTH)
+        wzs[j] = (wown[at, :] + wpair[at, :].astype(F32)).astype(BF16)
+
+        @pl.when(j != mf)
+        def _():
+            feat_copy(wzs.at[j], wz.at[mf], S_Z, j).start()
+
+        @pl.when(j == mf)
+        def _():
+            wz[mf] = wzs[j]
+
+    far_first(mf, nf, send_terms)
+
     def gathered(g, r):
         return nt(oh[rows_of(g), r * span : (r + 1) * span], chunk(loc2, r))
 
@@ -358,42 +374,23 @@
 
     await_blocks(loc2, S_G, nf - 1)
     lax.fori_loop(0, ny, pull_first, 0, unroll=True)
-
-    dom_copy(wsend, wpair, S_W, mate).wait_recv()
-
-    def send_terms(j):
-        at = pl.ds(pl.multiple_of(j * WIDTH, WIDTH), WIDTH)
-        wzs[j] = (wown[at, :] + wpair[at, :].astype(F32)).astype(BF16)
-
-        @pl.when(j != mf)
-        def _():
-            feat_copy(wzs.at[j], wz.at[mf], S_Z, j).start()
-
-        @pl.when(j == mf)
-        def _():
-            wz[mf] = wzs[j]
-
-    far_first(mf, nf, send_terms)
 
     await_blocks(loc2, S_G + 1, nf - 1)
     lax.fori_loop(0, ny, pull_second, 0, unroll=True)
     await_blocks(loc2, S_G + 2, nf - 1)
     far_first(my_y, ny, pull_last)
 
+    for c in range(width // TILE):
+        for r in range(3):
+            v = nn(w_ref[0, c * TILE : (c + 1) * TILE, :], pgrad[r]).astype(BF16)
+            ssend[2 * c, r] = v[:WIDTH]
+            ssend[2 * c + 1, r] = v[WIDTH:]
+    sgr[mf] = ssend[mf]
+
     def send_self_grad(j):
-        w = w_ref[0, pl.ds(pl.multiple_of(j * WIDTH, WIDTH), WIDTH), :]
-        for r in range(3):
-            ssend[j, r] = nn(w, pgrad[r]).astype(BF16)
-
         @pl.when(j != mf)
         def _():
             feat_copy(ssend.at[j], sgr.at[mf], S_S, j).start()
-
-        @pl.when(j == mf)
-        def _():
-            sgr[mf] = ssend[j]
-
-    far_first(mf, nf, send_self_grad)
 
     await_dom(2)
     mirrors_in(2, loc2)
@@ -416,6 +413,7 @@
     lax.fori_loop(1, chips, send_pieces, 0)
     wq[chip] = wps[chip]
 
+    far_first(mf, nf, send_self_grad)
     multiply(loc2, 5, False, tiles // 2, tiles, run)
     push(3, 5)
 

time: 86.3 us -> 85.8 us (level)
  no operation moved by 1% of the time
where the time goes in v4:
time: 85.8 us; the launch traced here: 85.7 us
  Pallas kernels  82.3 us (96%)
  local copies, waits for them, and re-layouts  2.2 us (3%)
  between operations  1.29 us (2%)
    pallas_call x1, Pallas kernels, local(): pl.pallas_call(functools.partial(kernel, n_dom, nf), out_shape=(jax.Shape...  82.3 us
    unnamed x3, local copies, waits for them, and re-layouts  2.2 us

profile of v4, /device:TPU:1, one launch (start us, length us, event | category | flops | bytes accessed | tf_op | source)
XLA Modules:
  0.0 85.7 jit_solution(3948327269140122828)
XLA Ops:
  1.3 82.3 %shard_map.94 = (bf16[512,384]{1,0:T(8,128)(2,1)S(1)}, bf16[64,3072]{1,0:T(8,128)(2,1)S(1)}, f32[2,64,512]{2,1,0:T(8,128)S(1)}) custom-call(bf16[64,3072]{1,0:T(8,128)(2,1)} %f_in.1, bf16[2,512,512]{2,1,0:T(8,128)(2,1)} %w_in.1, bf16[72,128,128]{2,1,0:T(8,128)(2,1)} %tile_in.1, s32[2,72]{1,0:T(2,128)} %bitcast.3, s32[1]{0:T(128)S(6)} %copy.13.tc_ref, ...), custom_call_target="tpu_custom_call" | custom-call | tf_op jit(solution)/shard_map/pallas_call | solution.py:476
  83.5 0.7 copy.14
  84.3 0.7 copy.15
  85.0 0.7 copy.16
